TPU v7x, 128 devices: a whole 4x4x4 slice. The times are simulated.
128 devices in a mesh: sec: 8 (over z_hi, y), op: 16 (over x, z_lo, core).
Axes of the slice: x: 4, y: 4, z: 4 (z_hi: 2, z_lo: 2; z = z_hi * 2 + z_lo), core: 2. Of those that a mesh axis runs over, the one named last changes fastest.
Arguments:
- state: float32 [8, 1024, 1024], P('sec'), may hold values from -6 to 6
- left_ops: float32 [16, 8, 1024, 1024], P('op', 'sec'), may hold values from -1 to 1
- right_ops: float32 [16, 8, 1024, 1024], P('op', 'sec'), may hold values from -1 to 1
- charge: int32 [16], P('op'), may hold values from -1 to 1, as said below
- sizes: int32 [8], P('sec'), may hold values from 64 to 1024, as said below
Outputs:
- next_vector: float32 [8, 1024, 1024], P('sec', 'op')
- next_sigma: float32 [8, 1024, 1024], P('sec', 'op')
- projected: float32 [2], replicated
Inputs may be any that keep to these rules, and one draw needn't show every extreme that they name: Each of -1, 0 and 1 is the charge of some operator. `sizes`: some sector holds exactly 1024 states and another exactly 64.
All inputs are finite; a program needn't handle non-finite values.
Results may differ from a plain program's by a relative error of at most 0.0003.
Values sent between devices are 32-bit elements; how exact they have to be, the bound alone decides.
A program may use at most 128 MiB of HBM per device.

v0:
```python
import jax
import jax.numpy as jnp
from jax import lax
from jax.sharding import PartitionSpec as P

epsilon = 1e-06


def passed_along(block, axis, distance):
    devices = range(lax.axis_size(axis))
    route = [(i - distance, i) for i in devices if i - distance in devices]
    return lax.ppermute(block, axis, route)


def local_terms(vector, left_ops, right_ops, charge):
    moved = jnp.einsum("sij,sjl->sil", left_ops[0], vector, precision=lax.Precision.HIGHEST)
    charge_now = charge[0]
    from_lower = passed_along(moved, "sec", 1)
    from_upper = passed_along(moved, "sec", -1)
    raised = jnp.concatenate([from_lower, moved[:-1]], axis=0)
    lowered = jnp.concatenate([moved[1:], from_upper], axis=0)
    shifted = jnp.where(charge_now == 1, raised, jnp.where(charge_now == -1, lowered, moved))
    total = jnp.einsum("til,tml->tim", shifted, right_ops[0], precision=lax.Precision.HIGHEST)
    return total


def on_device(state, left_ops, right_ops, charge, sizes):
    sec_local = state.shape[0]
    block_rows = state.shape[1]
    share_rows = block_rows // lax.axis_size("op")
    row_start = lax.axis_index("op") * share_rows
    cell_count = 1.0 * sec_local * lax.axis_size("sec") * block_rows * block_rows
    alive = (jnp.arange(block_rows, dtype=jnp.int32)[None, :] < sizes[:, None]).astype(jnp.float32)
    live_mask = alive[:, :, None] * alive[:, None, :]

    def own_rows(whole):
        return lax.dynamic_slice_in_dim(whole, row_start, share_rows, 1)

    def operator_total(vector):
        terms = local_terms(vector, left_ops, right_ops, charge)
        whole_sigma = lax.psum(terms, "op") * live_mask
        return (own_rows(whole_sigma), whole_sigma)

    start = state * live_mask
    start_share = own_rows(start)
    start_norm = lax.psum(jnp.sum(start_share * start_share), ("sec", "op"))
    first_scale = lax.rsqrt(start_norm / cell_count + epsilon)
    first_vector = start * first_scale
    first_share = own_rows(first_vector)
    sigma_share, sigma_whole = operator_total(first_vector)
    intersection = lax.psum(jnp.sum(first_share * sigma_share), ("sec", "op"))
    rayleigh_one = intersection / cell_count
    resid_share = sigma_share - rayleigh_one * first_share
    resid_square = lax.psum(jnp.sum(resid_share * resid_share), ("sec", "op"))
    next_scale = lax.rsqrt(resid_square / cell_count + epsilon)
    next_whole = (sigma_whole - rayleigh_one * first_vector) * next_scale
    next_share = own_rows(next_whole)
    next_sigma, unused = operator_total(next_whole)
    second_intersection = lax.psum(jnp.sum(next_share * next_sigma), ("sec", "op"))
    rayleigh_two = second_intersection / cell_count
    return (next_share, next_sigma, jnp.stack([rayleigh_one, rayleigh_two]))


def solution(mesh):
    in_specs = (
        P("sec", None, None),
        P("op", "sec", None, None),
        P("op", "sec", None, None),
        P("op"),
        P("sec"),
    )
    out_specs = (P("sec", "op", None), P("sec", "op", None), P())
    return jax.shard_map(
        on_device, mesh=mesh, in_specs=in_specs, out_specs=out_specs, check_vma=False
    )
```

profile of v0, /device:TPU:1, one launch (start us, length us, event | category | flops | bytes accessed | tf_op | source)
XLA Modules:
  0.0 879.5 jit_solution(7237900617677951572)
XLA Ops:
  7.2 0.0 all-reduce.3.cloned.1.call-start
  7.9 2.6 multiply_multiply_fusion.1
  10.5 0.7 multiply_reduce_fusion.3
  11.1 68.7 %psum.42 = f32[]{:T(128)} all-reduce(f32[]{:T(128)} %multiply_reduce_fusion.3), channel_id=1, replica_groups=mesh['sec'=8,'op'=16] {'sec','op'}, use_global_device_ids=true, to_apply=%region_1.0 | all-reduce | flops 1 | bytes 8 | tf_op jit(solution)/shard_map/psum | solution.py:46
  80.5 0.0 copy-start.5
  80.5 2.9 broadcast_multiply_fusion
  83.4 0.0 copy-start.3
  83.4 2.0 copy-done.3
  85.4 0.0 copy-done.5
  85.4 0.0 copy-start.1
  85.4 27.4 %fusion.16 = f32[1,1024,1024]{1,2,0:T(8,128)S(1)} fusion(f32[1,1,1024,1024]{3,2,1,0:T(8,128)S(1)} %copy-done.5, f32[1,1024,1024]{2,1,0:T(8,128)S(1)} %broadcast_multiply_fusion), kind=kOutput, calls=%fused_computation.19 | convolution fusion | flops 12884901888 | bytes 12582912 | tf_op jit(solution)/shard_map/sij,sjl->sil/dot_general | solution.py:16
  112.8 1.3 collective-permute-start.1
  114.1 4.3 collective-permute-start
  119.0 86.8 %collective-permute-done.1 = f32[1,1024,1024]{1,2,0:T(8,128)S(1)} collective-permute-done((f32[1,1024,1024]{1,2,0:T(8,128)S(1)}, f32[1,1024,1024]{1,2,0:T(8,128)S(1)}, u32[]{:S(2)}, u32[]{:S(2)}) %collective-permute-start.1) | collective-permute-done | bytes 4194336 | tf_op jit(solution)/shard_map/ppermute | solution.py:12
  205.9 0.9 collective-permute-done
  206.7 0.0 copy-done.1
  206.7 27.8 %fusion.21 = f32[1,1024,1024]{2,1,0:T(8,128)} fusion(f32[1,1,1024,1024]{3,2,1,0:T(8,128)S(1)} %copy-done.1, f32[1,1024,1024]{1,2,0:T(8,128)S(1)} %collective-permute-done, f32[1,1024,1024]{1,2,0:T(8,128)S(1)} %collective-permute-done.1, f32[1,1024,1024]{1,2,0:T(8,128)S(1)} %fusion.16, pred[]{:T(512)} %bitcast.6, pred[]{:T(512)} %bitcast), kind=kOutput, calls=%fused_computation.20 | convolution fusion | flops 12886999040 | bytes 20971522 | tf_op jit(solution)/shard_map/til,tml->tim/dot_general | solution.py:23
  234.6 0.0 all-reduce.3.cloned.1.call-update
  234.6 0.0 all-reduce.5.cloned.1.call-start
  234.7 134.9 %all-reduce.3.cloned.1.call-done = f32[1,1024,1024]{2,1,0:T(8,128)} async-done(((f32[1,1024,1024]{2,1,0:T(8,128)}), f32[1,1024,1024]{2,1,0:T(8,128)}) %all-reduce.3.cloned.1.call-update) | async-done | bytes 4194320 | tf_op jit(solution)/shard_map/psum | solution.py:41
  369.6 4.7 multiply_multiply_fusion
  374.3 0.0 copy-start
  374.3 2.0 copy-done
  376.3 1.6 multiply_reduce_fusion.2
  377.9 67.3 %psum.44 = f32[]{:T(128)} all-reduce(f32[]{:T(128)} %multiply_reduce_fusion.2), channel_id=1, replica_groups=mesh['sec'=8,'op'=16] {'sec','op'}, use_global_device_ids=true, to_apply=%region_4.5 | all-reduce | flops 1 | bytes 8 | tf_op jit(solution)/shard_map/psum | solution.py:51
  445.9 1.7 multiply_reduce_fusion.1
  447.6 62.6 %psum.45 = f32[]{:T(128)} all-reduce(f32[]{:T(128)} %multiply_reduce_fusion.1), channel_id=1, replica_groups=mesh['sec'=8,'op'=16] {'sec','op'}, use_global_device_ids=true, to_apply=%region_6.7 | all-reduce | flops 1 | bytes 8 | tf_op jit(solution)/shard_map/psum | solution.py:54
  510.9 0.0 copy-start.6
  510.9 4.5 subtract_multiply_fusion
  515.4 0.0 copy-start.4
  515.4 2.0 copy-done.4
  517.4 0.0 copy-done.6
  517.4 0.0 copy-start.2
  517.4 27.0 %fusion.26 = f32[1,1024,1024]{1,2,0:T(8,128)S(1)} fusion(f32[1,1,1024,1024]{3,2,1,0:T(8,128)S(1)} %copy-done.6, f32[1,1024,1024]{2,1,0:T(8,128)S(1)} %subtract_multiply_fusion), kind=kOutput, calls=%fused_computation.21 | convolution fusion | flops 12884901888 | bytes 12582912 | tf_op jit(solution)/shard_map/sij,sjl->sil/dot_general | solution.py:16
  544.5 1.3 collective-permute-start.3
  545.8 4.3 collective-permute-start.2
  550.0 87.9 %collective-permute-done.3 = f32[1,1024,1024]{1,2,0:T(8,128)S(1)} collective-permute-done((f32[1,1024,1024]{1,2,0:T(8,128)S(1)}, f32[1,1024,1024]{1,2,0:T(8,128)S(1)}, u32[]{:S(2)}, u32[]{:S(2)}) %collective-permute-start.3) | collective-permute-done | bytes 4194336 | tf_op jit(solution)/shard_map/ppermute | solution.py:12
  638.0 0.9 collective-permute-done.2
  638.8 0.0 copy-done.2
  638.8 27.7 %fusion.31 = f32[1,1024,1024]{2,1,0:T(8,128)} fusion(f32[1,1,1024,1024]{3,2,1,0:T(8,128)S(1)} %copy-done.2, f32[1,1024,1024]{1,2,0:T(8,128)S(1)} %collective-permute-done.2, f32[1,1024,1024]{1,2,0:T(8,128)S(1)} %collective-permute-done.3, f32[1,1024,1024]{1,2,0:T(8,128)S(1)} %fusion.26, pred[]{:T(512)} %bitcast.6, pred[]{:T(512)} %bitcast), kind=kOutput, calls=%fused_computation.22 | convolution fusion | flops 12886999040 | bytes 20971522 | tf_op jit(solution)/shard_map/til,tml->tim/dot_general | solution.py:23
  666.5 0.0 all-reduce.5.cloned.1.call-update
  666.5 134.8 %all-reduce.5.cloned.1.call-done = f32[1,1024,1024]{2,1,0:T(8,128)} async-done(((f32[1,1024,1024]{2,1,0:T(8,128)}), f32[1,1024,1024]{2,1,0:T(8,128)}) %all-reduce.5.cloned.1.call-update) | async-done | bytes 4194320 | tf_op jit(solution)/shard_map/psum | solution.py:41
  801.3 2.6 multiply_reduce_fusion
  803.9 67.3 %psum.47 = f32[]{:T(128)} all-reduce(f32[]{:T(128)} %get-tuple-element.3), channel_id=1, replica_groups=mesh['sec'=8,'op'=16] {'sec','op'}, use_global_device_ids=true, to_apply=%region_9.10 | all-reduce | flops 1 | bytes 8 | tf_op jit(solution)/shard_map/psum | solution.py:59
  871.8 0.6 pad_maximum_fusion
  (1 shorter events, 0.0 us)
Async XLA Ops:
  7.2 362.4 %all-reduce.3.cloned.1.call-start = ((), (), s32[]{:S(2)}) async-start(), calls=%async_computation | async-start | bytes 8388608 | tf_op jit(solution)/shard_map/psum | solution.py:41
  80.5 4.9 copy-start.5
  83.4 2.0 copy-start.3
  85.4 121.4 %copy-start.1 = (f32[1,1,1024,1024]{3,2,1,0:T(8,128)S(1)}, f32[1,1,1024,1024]{3,2,1,0:T(8,128)}, u32[]{:S(2)}) copy-start(f32[1,1,1024,1024]{3,2,1,0:T(8,128)} %param.7) | copy-start | bytes 12582916
  112.8 93.0 %collective-permute-start.1 = (f32[1,1024,1024]{1,2,0:T(8,128)S(1)}, f32[1,1024,1024]{1,2,0:T(8,128)S(1)}, u32[]{:S(2)}, u32[]{:S(2)}) collective-permute-start(f32[1,1024,1024]{1,2,0:T(8,128)S(1)} %fusion.16), channel_id=1, source_target_pairs={{16,0},{32,16},{48,32},{64,48},{80,64},{96,80},{112,96},{17,1},{33... | collective-permute-start | bytes 12582920 | tf_op jit(solution)/shard_map/ppermute | solution.py:12
  114.1 92.6 %collective-permute-start = (f32[1,1024,1024]{1,2,0:T(8,128)S(1)}, f32[1,1024,1024]{1,2,0:T(8,128)S(1)}, u32[]{:S(2)}, u32[]{:S(2)}) collective-permute-start(f32[1,1024,1024]{1,2,0:T(8,128)S(1)} %fusion.16), channel_id=1, source_target_pairs={{0,16},{16,32},{32,48},{48,64},{64,80},{80,96},{96,112},{1,17},{17... | collective-permute-start | bytes 12582920 | tf_op jit(solution)/shard_map/ppermute | solution.py:12
  234.6 566.7 %all-reduce.5.cloned.1.call-start = ((), (), s32[]{:S(2)}) async-start(), calls=%async_computation.1 | async-start | bytes 8388608 | tf_op jit(solution)/shard_map/psum | solution.py:41
  374.3 2.0 copy-start
  510.9 6.5 copy-start.6
  515.4 2.0 copy-start.4
  517.4 121.4 %copy-start.2 = (f32[1,1,1024,1024]{3,2,1,0:T(8,128)S(1)}, f32[1,1,1024,1024]{3,2,1,0:T(8,128)}, u32[]{:S(2)}) copy-start(f32[1,1,1024,1024]{3,2,1,0:T(8,128)} %param.7) | copy-start | bytes 12582916
  544.5 93.5 %collective-permute-start.3 = (f32[1,1024,1024]{1,2,0:T(8,128)S(1)}, f32[1,1024,1024]{1,2,0:T(8,128)S(1)}, u32[]{:S(2)}, u32[]{:S(2)}) collective-permute-start(f32[1,1024,1024]{1,2,0:T(8,128)S(1)} %fusion.26), channel_id=1, source_target_pairs={{16,0},{32,16},{48,32},{64,48},{80,64},{96,80},{112,96},{17,1},{33... | collective-permute-start | bytes 12582920 | tf_op jit(solution)/shard_map/ppermute | solution.py:12
  545.8 93.1 %collective-permute-start.2 = (f32[1,1024,1024]{1,2,0:T(8,128)S(1)}, f32[1,1024,1024]{1,2,0:T(8,128)S(1)}, u32[]{:S(2)}, u32[]{:S(2)}) collective-permute-start(f32[1,1024,1024]{1,2,0:T(8,128)S(1)} %fusion.26), channel_id=1, source_target_pairs={{0,16},{16,32},{32,48},{48,64},{64,80},{80,96},{96,112},{1,17},{17... | collective-permute-start | bytes 12582920 | tf_op jit(solution)/shard_map/ppermute | solution.py:12
Sparse Core Ops, SparseCore 0:
  234.7 134.8 all-reduce.2
  666.7 134.6 all-reduce.4
where the time goes:
time: 883 us; the launch traced here: 879 us
  waiting for transfers between devices  446 us (51%)
  blocking collectives  266 us (30%)
  matrix products  110 us (12%)
  other arithmetic  21.9 us (2%)
  between operations  18.4 us (2%)
  starting transfers between devices  11.2 us (1%)
    psum x2, waiting for transfers between devices, operator_total(): whole_sigma = lax.psum(terms, 'op') * live_mask  270 us
    ppermute x4, waiting for transfers between devices, passed_along(): return lax.ppermute(block, axis, route)  177 us
    psum x1, blocking collectives, on_device(): start_norm = lax.psum(jnp.sum(start_share * start_share), ('sec', 'op'))  68.7 us
    psum x1, blocking collectives, on_device(): intersection = lax.psum(jnp.sum(first_share * sigma_share), ('sec', 'op'))  67.3 us
    psum x1, blocking collectives, on_device(): lax.psum(jnp.sum(next_share * next_sigma), ('sec', 'op'))  67.3 us
    psum x1, blocking collectives, on_device(): resid_square = lax.psum(jnp.sum(resid_share * resid_share), ('sec', 'op'))  62.6 us
    dot_general x2, matrix products, local_terms(): jnp.einsum('til,tml->tim', shifted, right_ops[0], precision=lax.Precision...  55.5 us
    dot_general x2, matrix products, local_terms(): jnp.einsum('sij,sjl->sil', left_ops[0], vector, precision=lax.Precision.H...  54.5 us
  transfers between devices with their start and end apart: 6, of which 6 were waited for; matrix products, arithmetic and copies ran while one was open for 0% of the time, Pallas kernels for 0%

commit v1 on v0

v1 whole, which is shorter than its diff:
```python
import functools
import jax
import jax.numpy as jnp
from jax import lax
from jax.experimental import pallas as pl
from jax.experimental.pallas import tpu as pltpu
from jax.sharding import PartitionSpec as P

epsilon = 1e-06
CHUNKS = 4
F32 = jnp.float32
BF16 = jnp.bfloat16
MESH = pl.DeviceIdType.MESH


def split(x):
    high = x.astype(BF16)
    return high, (x - high.astype(F32)).astype(BF16)


def dot3(a_high, a_low, b_high, b_low, contract):
    def one(a, b):
        return lax.dot_general(a, b, (contract, ((), ())), preferred_element_type=F32)
    return one(a_high, b_high) + (one(a_high, b_low) + one(a_low, b_high))


def kernel(
    nq, ns, state_ref, l_ref, r_ref, charge_ref, sizes_ref,
    nv_ref, out_sigma_ref, proj_ref,
    l_high, l_low, v_high, v_low, p_high, p_low, x_own, x_sent, x_got,
    y_out, y_got, t_out, t_got, sig, gathered, klass, tile_out, op_got, sec_got,
    x_send, x_recv, y_send, y_recv, t_send, t_recv, g_send, g_recv,
    k_send, k_recv, op_send, op_recv, sec_send, sec_recv,
):
    no, share, n = state_ref.shape
    rq, cq = share // nq, n // nq
    s = lax.axis_index("sec")
    k = lax.axis_index("op")
    core = k % 2
    zlo = (k // 2) % 2
    x = k // 4
    nx = no // 4
    d = 1 - 2 * core
    dst, src = s + d, s - d
    has_dst = (dst >= 0) & (dst < ns)
    has_src = (src >= 0) & (src < ns)
    has_up = s < ns - 1
    has_down = s > 0
    charge = charge_ref[0]
    size = sizes_ref[0]
    cells = 1.0 * ns * n * n
    crossed = charge == -d

    barrier = pltpu.get_barrier_semaphore()

    def greet_op(j, carry):
        pl.semaphore_signal(barrier, inc=1, device_id=(s, (k + j) % no), device_id_type=MESH)
        return carry

    def greet_sec(j, carry):
        pl.semaphore_signal(barrier, inc=1, device_id=((s + j) % ns, k), device_id_type=MESH)
        return carry

    lax.fori_loop(1, no, greet_op, 0)
    lax.fori_loop(1, ns, greet_sec, 0)

    def op_copy(source, target, send, recv, j):
        return pltpu.make_async_remote_copy(
            src_ref=source, dst_ref=target.at[j], send_sem=send, recv_sem=recv,
            device_id=(s, (k + j) % no), device_id_type=MESH)

    def sec_copy(source, target, send, recv, j):
        return pltpu.make_async_remote_copy(
            src_ref=source, dst_ref=target.at[j], send_sem=send, recv_sem=recv,
            device_id=((s + j) % ns, k), device_id_type=MESH)

    def wait_many(target, send, recv, count):
        whole = target.at[pl.ds(1, count - 1)]
        copy = pltpu.make_async_remote_copy(
            src_ref=whole, dst_ref=whole, send_sem=send, recv_sem=recv,
            device_id=(s, (k + 1) % no), device_id_type=MESH)
        copy.wait_send()
        copy.wait_recv()

    def op_start(which, value):
        op_got[which, 0] = jnp.full((8, 128), value, F32)

        def body(j, carry):
            op_copy(op_got.at[which, 0], op_got.at[which], op_send.at[which], op_recv.at[which], j).start()
            return carry
        lax.fori_loop(1, no, body, 0)

    def op_finish(which):
        wait_many(op_got.at[which], op_send.at[which], op_recv.at[which], no)
        total = jnp.zeros((8, 128), F32)
        for i in range(no):
            total = total + op_got[which, (k + no - i) % no]
        return total

    def sec_start(which, tile):
        sec_got[which, 0] = tile

        def body(j, carry):
            sec_copy(sec_got.at[which, 0], sec_got.at[which], sec_send.at[which], sec_recv.at[which], j).start()
            return carry
        lax.fori_loop(1, ns, body, 0)

    def sec_finish(which):
        wait_many(sec_got.at[which], sec_send.at[which], sec_recv.at[which], ns)
        total = jnp.zeros((8, 128), F32)
        for i in range(ns):
            total = total + sec_got[which, (s + ns - i) % ns]
        return total

    def shifted(source, q):
        return pltpu.make_async_remote_copy(
            src_ref=source.at[q], dst_ref=x_got.at[q], send_sem=x_send.at[q], recv_sem=x_recv.at[q],
            device_id=((dst + ns) % ns, k), device_id_type=MESH)

    columns = lax.broadcasted_iota(jnp.int32, (share, n), 1) < size
    rows = lax.broadcasted_iota(jnp.int32, (share, n), 0)

    def live(block):
        return columns & (rows + block * share < size)

    def start_block(block):
        return jnp.where(live(block), state_ref[block], 0.0)

    def fill_start(block, total):
        value = start_block(block)
        at = pl.ds(pl.multiple_of(block * share, share), share)
        v_high[at], v_low[at] = split(value)
        return total + jnp.sum((value * value).reshape(share // 8, 8, n), axis=0)

    squares = lax.fori_loop(0, no, fill_start, jnp.zeros((8, n), F32))
    start_square = jnp.sum(squares)

    @pl.when(jnp.logical_not(has_src))
    def _():
        x_got[...] = jnp.zeros_like(x_got)

    @pl.when(jnp.logical_not(has_up))
    def _():
        t_got[0] = jnp.zeros(t_got.shape[1:], F32)

    @pl.when(jnp.logical_not(has_down))
    def _():
        t_got[1] = jnp.zeros(t_got.shape[1:], F32)

    pl.semaphore_wait(barrier, no - 1 + ns - 1)

    klass[0] = jnp.full((8, 128), jnp.where(crossed, charge, 0), jnp.int32).astype(F32)

    def klass_body(j, carry):
        op_copy(klass.at[0], klass, k_send, k_recv, j).start()
        return carry
    lax.fori_loop(1, no, klass_body, 0)
    sec_start(0, jnp.full((8, 128), start_square, F32))

    def left_products(first):
        def body(q, carry):
            if first:
                at = pl.ds(pl.multiple_of(q * rq, rq), rq)
                high, low = split(l_ref[:, at, :].reshape(no * rq, n))
                l_high[q] = high
                l_low[q] = low
            else:
                high, low = l_high[q], l_low[q]
            product = dot3(high, low, v_high[...], v_low[...], ((1,), (0,)))
            x_own[q] = product
            if first:
                right = r_ref[q]
                x_sent[q] = jnp.where(charge == d, product, right)
                p_high[q], p_low[q] = split(jnp.where(crossed, product, right))

            @pl.when(has_dst)
            def _():
                shifted(x_sent if first else x_own, q).start()
            return carry
        lax.fori_loop(0, nq, body, 0)

    def t_copy(way, q):
        to = s - 1 if way == 0 else s + 1
        return pltpu.make_async_remote_copy(
            src_ref=t_out.at[way, q], dst_ref=t_got.at[way, q], send_sem=t_send.at[way, q],
            recv_sem=t_recv.at[way, q], device_id=((to + ns) % ns, k), device_id_type=MESH)

    def weight(j, which):
        w = (klass[j] == which).astype(F32)
        return jnp.concatenate([w] * (cq // 128), axis=1)[None]

    def reduce_chunk(q):
        wait_many(y_got.at[q], y_send.at[q], y_recv.at[q], no)

        def body(j, totals):
            part = y_got[q, j].reshape(share // 8, 8, cq)
            return tuple(t + part * weight(j, w) for t, w in zip(totals, (0.0, -1.0, 1.0)))

        own = y_out[q, k].reshape(share // 8, 8, cq)
        totals = tuple(own * weight(0, w) for w in (0.0, -1.0, 1.0))
        totals = lax.fori_loop(1, no, body, totals)
        here, below, above = (t.reshape(share, cq) for t in totals)
        at = pl.ds(pl.multiple_of(q * rq, rq), rq)
        for p in range(nq):
            sig[at, p * cq:(p + 1) * cq] = here[p * rq:(p + 1) * rq]
        t_out[0, q] = below
        t_out[1, q] = above

        @pl.when(has_down)
        def _():
            t_copy(0, q).start()

        @pl.when(has_up)
        def _():
            t_copy(1, q).start()

    def right_products(first):
        def body(q, carry):
            @pl.when(has_src)
            def _():
                shifted(x_sent, q).wait_recv()
            use_own = charge == 0 if first else charge != d
            high, low = split(jnp.where(use_own, x_own[q], x_got[q]))
            for p in range(nq):
                block = dot3(high, low, p_high[p], p_low[p], ((1,), (1,)))
                if first:
                    block = jnp.where(crossed, block.T, block)
                y_out[q, :, p * rq:(p + 1) * rq, :] = block.reshape(no, rq, cq)

            def send(j, carry):
                to = (k + j) % no
                op_copy(y_out.at[q, to], y_got.at[q], y_send.at[q], y_recv.at[q], j).start()
                return carry
            lax.fori_loop(1, no, send, 0)

            @pl.when(q > 0)
            def _():
                reduce_chunk(q - 1)
            return carry
        lax.fori_loop(0, nq, body, 0)

        @pl.when(has_dst)
        def _():
            def done(q, carry):
                shifted(x_sent if first else x_own, q).wait_send()
                return carry
            lax.fori_loop(0, nq, done, 0)
        if first:
            def keep(q, carry):
                p_high[q], p_low[q] = split(jnp.where(crossed, x_got[q], r_ref[q]))
                return carry
            lax.fori_loop(0, nq, keep, 0)
        reduce_chunk(nq - 1)

    def neighbours_in(first):
        def body(q, carry):
            @pl.when(has_up)
            def _():
                t_copy(0, q).wait_recv()

            @pl.when(has_down)
            def _():
                t_copy(1, q).wait_recv()

            @pl.when(has_down)
            def _():
                t_copy(0, q).wait_send()

            @pl.when(has_up)
            def _():
                t_copy(1, q).wait_send()
            return carry
        lax.fori_loop(0, nq, body, 0)
        for q in range(nq):
            both = t_got[0, q] + t_got[1, q]
            if first:
                sig[:, q * cq:(q + 1) * cq] += both
            else:
                for p in range(nq):
                    sig[q * rq:(q + 1) * rq, p * cq:(p + 1) * cq] += both[p * rq:(p + 1) * rq]
        return jnp.where(live(k), sig[...], 0.0)

    left_products(True)
    wait_many(klass, k_send, k_recv, no)
    right_products(True)
    sigma = neighbours_in(True)

    gathered[k] = sigma

    def member(dx, dz, dc):
        return ((x + dx) % nx) * 4 + ((zlo + dz) % 2) * 2 + (core + dc) % 2

    def g_copy(dx, dz, dc, to_x, to_z, to_c):
        block = gathered.at[member(nx - dx, dz, dc)]
        slot = ((dx + to_x) % nx) * 4 + ((dz + to_z) % 2) * 2 + (dc + to_c) % 2
        return pltpu.make_async_remote_copy(
            src_ref=block, dst_ref=block, send_sem=g_send.at[slot], recv_sem=g_recv.at[slot],
            device_id=(s, member(to_x, to_z, to_c)), device_id_type=MESH)

    def g_wait(dx, dz, dc):
        block = gathered.at[member(nx - dx, dz, dc)]
        slot = dx * 4 + dz * 2 + dc
        pltpu.make_async_remote_copy(
            src_ref=block, dst_ref=block, send_sem=g_send.at[slot], recv_sem=g_recv.at[slot],
            device_id=(s, member(0, 0, 1)), device_id_type=MESH).wait_recv()

    sends = []

    def g_start(*arguments):
        copy = g_copy(*arguments)
        copy.start()
        sends.append(copy)

    around = [1, nx - 1] + list(range(2, nx - 1))
    g_start(0, 0, 0, 0, 1, 0)
    for step in around:
        g_start(0, 0, 0, step, 0, 0)
    g_start(0, 0, 0, 0, 0, 1)
    op_start(0, jnp.sum(sigma * start_block(k)))
    g_wait(0, 1, 0)
    for step in around:
        g_start(0, 1, 0, step, 0, 0)
    g_start(0, 1, 0, 0, 0, 1)
    sec_start(1, op_finish(0))
    for dz in (0, 1):
        for dx in around:
            g_wait(dx, dz, 0)
            g_start(dx, dz, 0, 0, 0, 1)
    start_total = sec_finish(0)
    cross_total = sec_finish(1)
    scale = lax.rsqrt(start_total / cells + epsilon)
    rayleigh_one = cross_total * (scale * scale) / cells
    shift_by = jnp.max(rayleigh_one)
    for dz in (0, 1):
        for dx in range(nx):
            g_wait(dx, dz, 1)
    for copy in sends:
        copy.wait_send()

    def residual_block(block):
        return gathered[block] - shift_by * start_block(block)

    def fill_residual(block, total):
        value = residual_block(block)
        at = pl.ds(pl.multiple_of(block * share, share), share)
        v_high[at], v_low[at] = split(value)
        return total + jnp.sum((value * value).reshape(share // 8, 8, n), axis=0)

    squares = lax.fori_loop(0, no, fill_residual, jnp.zeros((8, n), F32))
    sec_start(2, jnp.full((8, 128), jnp.sum(squares), F32))

    left_products(False)
    right_products(False)
    residual_total = sec_finish(2)
    next_tile = scale * lax.rsqrt(residual_total * (scale * scale) / cells + epsilon)
    next_scale = jnp.max(next_tile)
    sigma = neighbours_in(False)
    residual = residual_block(k)
    op_start(1, jnp.sum(sigma * residual))
    nv_ref[0] = residual * next_scale
    out_sigma_ref[0] = sigma * next_scale
    sec_start(3, op_finish(1))
    rayleigh_two = sec_finish(3) * (next_tile * next_tile) / cells
    lane = lax.broadcasted_iota(jnp.int32, (8, 128), 1)
    proj_ref[...] = jnp.where(lane == 0, rayleigh_one, rayleigh_two)


def on_device(ns, state, left_ops, right_ops, charge, sizes):
    n = state.shape[1]
    no = lax.axis_size("op")
    share = n // no
    nq = CHUNKS
    rq, cq = share // nq, n // nq
    vmem = pltpu.VMEM
    dma = pltpu.SemaphoreType.DMA
    whole = pl.BlockSpec(memory_space=vmem)
    small = pl.BlockSpec(memory_space=pltpu.SMEM)
    nv, sigma, proj = pl.pallas_call(
        functools.partial(kernel, nq, ns),
        out_shape=[
            jax.ShapeDtypeStruct((1, share, n), F32),
            jax.ShapeDtypeStruct((1, share, n), F32),
            jax.ShapeDtypeStruct((8, 128), F32),
        ],
        in_specs=[whole, whole, whole, small, small],
        out_specs=[whole, whole, whole],
        scratch_shapes=[
            vmem((nq, cq, n), BF16), vmem((nq, cq, n), BF16),
            vmem((n, n), BF16), vmem((n, n), BF16),
            vmem((nq, cq, n), BF16), vmem((nq, cq, n), BF16),
            vmem((nq, cq, n), F32), vmem((nq, cq, n), F32), vmem((nq, cq, n), F32),
            vmem((nq, no, share, cq), F32), vmem((nq, no, share, cq), F32),
            vmem((2, nq, share, cq), F32), vmem((2, nq, share, cq), F32),
            vmem((share, n), F32), vmem((no, share, n), F32),
            vmem((no, 8, 128), F32), vmem((8, 128), F32),
            vmem((2, no, 8, 128), F32), vmem((4, ns, 8, 128), F32),
            dma((nq,)), dma((nq,)), dma((nq,)), dma((nq,)),
            dma((2, nq)), dma((2, nq)), dma((no,)), dma((no,)),
            dma, dma, dma((2,)), dma((2,)), dma((4,)), dma((4,)),
        ],
        compiler_params=pltpu.CompilerParams(
            collective_id=0, has_side_effects=True, vmem_limit_bytes=60 * 1024 * 1024),
        cost_estimate=pl.CostEstimate(flops=24 * n * n * n, bytes_accessed=12 * n * n, transcendentals=0),
    )(state.reshape(no, share, n), left_ops.reshape(no, share, n), right_ops.reshape(nq, cq, n), charge, sizes)
    return nv, sigma, proj[0, :2]


def solution(mesh):
    in_specs = (
        P("sec", None, None),
        P("op", "sec", None, None),
        P("op", "sec", None, None),
        P("op"),
        P("sec"),
    )
    out_specs = (P("sec", "op", None), P("sec", "op", None), P())
    return jax.shard_map(
        functools.partial(on_device, mesh.shape["sec"]), mesh=mesh, in_specs=in_specs, out_specs=out_specs,
        check_vma=False)
```

time: 883 us -> 268 us (0.30)
  waiting for transfers between devices: 446 us -> 0 us
  blocking collectives: 266 us -> 0 us
  Pallas kernels: 0 us -> 261 us
  matrix products: 110 us -> 0 us
  other arithmetic: 21.9 us -> 0 us
  between operations: 18.4 us -> 1.93 us
  starting transfers between devices: 11.2 us -> 0 us
    psum x2 -> x0, waiting for transfers between devices: 270 us -> none  [operator_total(): whole_sigma = lax.psum(terms, 'op') * live_mask]
    psum x4 -> x0, blocking collectives: 266 us -> none  [the longest x1 68.7 us: on_device(): start_norm = lax.psum(jnp.sum(start_share * start_share), ('sec', 'op'))]
    pallas_call x0 -> x1, Pallas kernels: none -> 261 us  [on_device(): pl.pallas_call(functools.partial(kernel, nq, ns), out_shape=[jax.ShapeDty...]
    ppermute x4 -> x0, waiting for transfers between devices: 177 us -> none  [passed_along(): return lax.ppermute(block, axis, route)]
    dot_general x4 -> x0, matrix products: 110 us -> none  [the longest x2 55.5 us: local_terms(): jnp.einsum('til,tml->tim', shifted, right_ops[0], precision=lax.Precision...]
    mul x4 -> x0, other arithmetic: 14.7 us -> none  [the longest x1 4.72 us: operator_total(): whole_sigma = lax.psum(terms, 'op') * live_mask]
    ppermute x4 -> x0, starting transfers between devices: 11.1 us -> none  [passed_along(): return lax.ppermute(block, axis, route)]
  transfers between devices with their start and end apart: 6 -> 0, of which waited for: 6 -> 0; matrix products, arithmetic and copies ran while one was open for 0% -> 0% of each run, Pallas kernels for 0% -> 0%
where the time goes in v1:
time: 268 us; the launch traced here: 267 us
  Pallas kernels  261 us (97%)
  local copies, waits for them, and re-layouts  4.53 us (2%)
    pallas_call x1, Pallas kernels, on_device(): pl.pallas_call(functools.partial(kernel, nq, ns), out_shape=[jax.ShapeDty...  261 us

profile of v1, /device:TPU:1, one launch (start us, length us, event | category | flops | bytes accessed | tf_op | source)
XLA Modules:
  0.0 267.4 jit_solution(8260952113195108623)
XLA Ops:
  1.9 260.9 %shard_map.76 = (f32[1,64,1024]{2,1,0:T(8,128)}, f32[1,64,1024]{2,1,0:T(8,128)}, f32[8,128]{1,0:T(8,128)}) custom-call(f32[16,64,1024]{2,1,0:T(8,128)} %bitcast.5, f32[16,64,1024]{2,1,0:T(8,128)} %bitcast.6, f32[4,256,1024]{2,1,0:T(8,128)} %bitcast.7, s32[1]{0:T(128)S(6)} %copy.10.charge_ref, s32[1]{0:T(128)S(6)} %copy.11.sizes_ref), custom_call_target="tpu_custom_call" | custom-call | flops 25769803776 | bytes 12582912 | tf_op jit(solution)/shard_map/pallas_call | solution.py:378
  262.9 1.2 slice_bitcast_fusion
  264.0 1.7 copy.12
  265.7 1.7 copy.13

commit v2 on v1

--- a/solution.py
+++ b/solution.py
@@ -28,8 +28,8 @@
     nq, ns, state_ref, l_ref, r_ref, charge_ref, sizes_ref,
     nv_ref, out_sigma_ref, proj_ref,
     l_high, l_low, v_high, v_low, p_high, p_low, x_own, x_sent, x_got,
-    y_out, y_got, t_out, t_got, sig, gathered, klass, tile_out, op_got, sec_got,
-    x_send, x_recv, y_send, y_recv, t_send, t_recv, g_send, g_recv,
+    x_relay, y_out, y_got, z_out, z_got, t_out, t_got, sig, gathered, klass, op_got, sec_got,
+    x_send, x_recv, w_send, w_recv, y_send, y_recv, z_send, z_recv, t_send, t_recv, g_send, g_recv,
     k_send, k_recv, op_send, op_recv, sec_send, sec_recv,
 ):
     no, share, n = state_ref.shape
@@ -64,6 +64,16 @@
     lax.fori_loop(1, no, greet_op, 0)
     lax.fori_loop(1, ns, greet_sec, 0)
 
+    def member(dx, dz, dc):
+        return ((x + dx) % nx) * 4 + ((zlo + dz) % 2) * 2 + (core + dc) % 2
+
+    def greet_across(j, carry):
+        to = ((s + j) % ns, member(0, 1, 0))
+        pl.semaphore_signal(barrier, inc=1, device_id=to, device_id_type=MESH)
+        return carry
+
+    lax.fori_loop(1, ns, greet_across, 0)
+
     def op_copy(source, target, send, recv, j):
         return pltpu.make_async_remote_copy(
             src_ref=source, dst_ref=target.at[j], send_sem=send, recv_sem=recv,
@@ -117,6 +127,31 @@
             src_ref=source.at[q], dst_ref=x_got.at[q], send_sem=x_send.at[q], recv_sem=x_recv.at[q],
             device_id=((dst + ns) % ns, k), device_id_type=MESH)
 
+    half = ns // 2
+    at_edge = s == half - 1 + core
+    relays = s == (ns - 1) * (1 - core)
+
+    def to_relay(source, q):
+        return pltpu.make_async_remote_copy(
+            src_ref=source.at[q], dst_ref=x_relay.at[q // 2], send_sem=x_send.at[q], recv_sem=w_recv.at[q // 2],
+            device_id=((ns - 1) * (1 - core), member(0, 1, 0)), device_id_type=MESH)
+
+    def from_relay(q):
+        return pltpu.make_async_remote_copy(
+            src_ref=x_relay.at[q // 2], dst_ref=x_got.at[q], send_sem=w_send.at[q // 2], recv_sem=x_recv.at[q],
+            device_id=(half - core, member(0, 1, 0)), device_id_type=MESH)
+
+    def start_shift(source, q):
+        by_relay = at_edge & (q % 2 == 1)
+
+        @pl.when(by_relay)
+        def _():
+            to_relay(source, q).start()
+
+        @pl.when(has_dst & jnp.logical_not(by_relay))
+        def _():
+            shifted(source, q).start()
+
     columns = lax.broadcasted_iota(jnp.int32, (share, n), 1) < size
     rows = lax.broadcasted_iota(jnp.int32, (share, n), 0)
 
@@ -147,14 +182,17 @@
     def _():
         t_got[1] = jnp.zeros(t_got.shape[1:], F32)
 
-    pl.semaphore_wait(barrier, no - 1 + ns - 1)
-
-    klass[0] = jnp.full((8, 128), jnp.where(crossed, charge, 0), jnp.int32).astype(F32)
-
-    def klass_body(j, carry):
-        op_copy(klass.at[0], klass, k_send, k_recv, j).start()
-        return carry
-    lax.fori_loop(1, no, klass_body, 0)
+    pl.semaphore_wait(barrier, no - 1 + 2 * (ns - 1))
+
+    klass[0] = jnp.full((8, 128), jnp.where(crossed, 1.0, 0.0), F32)
+
+    def x_copy(source, target, send, recv, j):
+        return pltpu.make_async_remote_copy(
+            src_ref=source, dst_ref=target.at[j], send_sem=send, recv_sem=recv,
+            device_id=(s, member(j, 0, 0)), device_id_type=MESH)
+
+    for j in range(1, nx):
+        x_copy(klass.at[0], klass, k_send, k_recv, j).start()
     sec_start(0, jnp.full((8, 128), start_square, F32))
 
     def left_products(first):
@@ -173,9 +211,7 @@
                 x_sent[q] = jnp.where(charge == d, product, right)
                 p_high[q], p_low[q] = split(jnp.where(crossed, product, right))
 
-            @pl.when(has_dst)
-            def _():
-                shifted(x_sent if first else x_own, q).start()
+            start_shift(x_sent if first else x_own, q)
             return carry
         lax.fori_loop(0, nq, body, 0)
 
@@ -185,26 +221,37 @@
             src_ref=t_out.at[way, q], dst_ref=t_got.at[way, q], send_sem=t_send.at[way, q],
             recv_sem=t_recv.at[way, q], device_id=((to + ns) % ns, k), device_id_type=MESH)
 
-    def weight(j, which):
-        w = (klass[j] == which).astype(F32)
-        return jnp.concatenate([w] * (cq // 128), axis=1)[None]
-
-    def reduce_chunk(q):
-        wait_many(y_got.at[q], y_send.at[q], y_recv.at[q], no)
-
-        def body(j, totals):
-            part = y_got[q, j].reshape(share // 8, 8, cq)
-            return tuple(t + part * weight(j, w) for t, w in zip(totals, (0.0, -1.0, 1.0)))
-
-        own = y_out[q, k].reshape(share // 8, 8, cq)
-        totals = tuple(own * weight(0, w) for w in (0.0, -1.0, 1.0))
-        totals = lax.fori_loop(1, no, body, totals)
-        here, below, above = (t.reshape(share, cq) for t in totals)
+    def reduce_x(q):
+        wait_many(y_got.at[q], y_send.at[q], y_recv.at[q], nx)
+        flags = [jnp.concatenate([klass[j]] * (cq // 128), axis=1)[None] for j in range(nx)]
+        for m in range(4):
+            parts = [y_out[q, x * 4 + m]] + [y_got[q, j, m] for j in range(1, nx)]
+            parts = [part.reshape(share // 8, 8, cq) for part in parts]
+            there = [part * flag for part, flag in zip(parts, flags)]
+            here = [part - one for part, one in zip(parts, there)]
+            z_out[q, m, 0] = sum(here[1:], here[0]).reshape(share, cq)
+            z_out[q, m, 1] = sum(there[1:], there[0]).reshape(share, cq)
+        for j in range(1, 4):
+            z_copy(q, j).start()
+
+    def z_copy(q, j):
+        to = (k % 4 + j) % 4
+        return pltpu.make_async_remote_copy(
+            src_ref=z_out.at[q, to], dst_ref=z_got.at[q, j], send_sem=z_send.at[q], recv_sem=z_recv.at[q],
+            device_id=(s, x * 4 + to), device_id_type=MESH)
+
+    def reduce_z(q):
+        wait_many(z_got.at[q], z_send.at[q], z_recv.at[q], 4)
+        own = z_out[q, k % 4]
+        got = [z_got[q, j] for j in range(1, 4)]
+        here = (own[0] + got[1][0]) + (got[0][0] + got[2][0])
+        same = own[1] + got[1][1]
+        other = got[0][1] + got[2][1]
         at = pl.ds(pl.multiple_of(q * rq, rq), rq)
         for p in range(nq):
             sig[at, p * cq:(p + 1) * cq] = here[p * rq:(p + 1) * rq]
-        t_out[0, q] = below
-        t_out[1, q] = above
+        t_out[0, q] = jnp.where(core == 0, same, other)
+        t_out[1, q] = jnp.where(core == 0, other, same)
 
         @pl.when(has_down)
         def _():
@@ -216,6 +263,11 @@
 
     def right_products(first):
         def body(q, carry):
+            @pl.when(relays & (q % 2 == 1))
+            def _():
+                to_relay(x_sent, q).wait_recv()
+                from_relay(q).start()
+
             @pl.when(has_src)
             def _():
                 shifted(x_sent, q).wait_recv()
@@ -227,15 +279,17 @@
                     block = jnp.where(crossed, block.T, block)
                 y_out[q, :, p * rq:(p + 1) * rq, :] = block.reshape(no, rq, cq)
 
-            def send(j, carry):
-                to = (k + j) % no
-                op_copy(y_out.at[q, to], y_got.at[q], y_send.at[q], y_recv.at[q], j).start()
-                return carry
-            lax.fori_loop(1, no, send, 0)
+            for j in range(1, nx):
+                block = y_out.at[q, pl.ds(((x + j) % nx) * 4, 4)]
+                x_copy(block, y_got.at[q], y_send.at[q], y_recv.at[q], j).start()
 
             @pl.when(q > 0)
             def _():
-                reduce_chunk(q - 1)
+                reduce_x(q - 1)
+
+            @pl.when(q > 1)
+            def _():
+                reduce_z(q - 2)
             return carry
         lax.fori_loop(0, nq, body, 0)
 
@@ -245,12 +299,21 @@
                 shifted(x_sent if first else x_own, q).wait_send()
                 return carry
             lax.fori_loop(0, nq, done, 0)
+
+        @pl.when(relays)
+        def _():
+            def passed(i, carry):
+                from_relay(2 * i + 1).wait_send()
+                return carry
+            lax.fori_loop(0, nq // 2, passed, 0)
         if first:
             def keep(q, carry):
                 p_high[q], p_low[q] = split(jnp.where(crossed, x_got[q], r_ref[q]))
                 return carry
             lax.fori_loop(0, nq, keep, 0)
-        reduce_chunk(nq - 1)
+        reduce_x(nq - 1)
+        reduce_z(nq - 2)
+        reduce_z(nq - 1)
 
     def neighbours_in(first):
         def body(q, carry):
@@ -281,14 +344,11 @@
         return jnp.where(live(k), sig[...], 0.0)
 
     left_products(True)
-    wait_many(klass, k_send, k_recv, no)
+    wait_many(klass, k_send, k_recv, nx)
     right_products(True)
     sigma = neighbours_in(True)
 
     gathered[k] = sigma
-
-    def member(dx, dz, dc):
-        return ((x + dx) % nx) * 4 + ((zlo + dz) % 2) * 2 + (core + dc) % 2
 
     def g_copy(dx, dz, dc, to_x, to_z, to_c):
         block = gathered.at[member(nx - dx, dz, dc)]
@@ -389,11 +449,14 @@
             vmem((n, n), BF16), vmem((n, n), BF16),
             vmem((nq, cq, n), BF16), vmem((nq, cq, n), BF16),
             vmem((nq, cq, n), F32), vmem((nq, cq, n), F32), vmem((nq, cq, n), F32),
-            vmem((nq, no, share, cq), F32), vmem((nq, no, share, cq), F32),
+            vmem((nq // 2, cq, n), F32),
+            vmem((nq, no, share, cq), F32), vmem((nq, no // 4, 4, share, cq), F32),
+            vmem((nq, 4, 2, share, cq), F32), vmem((nq, 4, 2, share, cq), F32),
             vmem((2, nq, share, cq), F32), vmem((2, nq, share, cq), F32),
             vmem((share, n), F32), vmem((no, share, n), F32),
-            vmem((no, 8, 128), F32), vmem((8, 128), F32),
+            vmem((no // 4, 8, 128), F32),
             vmem((2, no, 8, 128), F32), vmem((4, ns, 8, 128), F32),
+            dma((nq,)), dma((nq,)), dma((nq // 2,)), dma((nq // 2,)),
             dma((nq,)), dma((nq,)), dma((nq,)), dma((nq,)),
             dma((2, nq)), dma((2, nq)), dma((no,)), dma((no,)),
             dma, dma, dma((2,)), dma((2,)), dma((4,)), dma((4,)),

time: 268 us -> 209 us (0.78)
  Pallas kernels: 261 us -> 203 us
    pallas_call x1, Pallas kernels: 261 us -> 203 us  [on_device(): pl.pallas_call(functools.partial(kernel, nq, ns), out_shape=[jax.ShapeDty...]
where the time goes in v2:
time: 209 us
  Pallas kernels  203 us (97%)
  local copies, waits for them, and re-layouts  4.53 us (2%)
    pallas_call x1, Pallas kernels, on_device(): pl.pallas_call(functools.partial(kernel, nq, ns), out_shape=[jax.ShapeDty...  203 us

profile of v2, /device:TPU:1, one launch (start us, length us, event | category | flops | bytes accessed | tf_op | source)
XLA Modules:
  0.0 209.0 jit_solution(6807901767174653552)
XLA Ops:
  1.9 202.5 %shard_map.76 = (f32[1,64,1024]{2,1,0:T(8,128)}, f32[1,64,1024]{2,1,0:T(8,128)}, f32[8,128]{1,0:T(8,128)}) custom-call(f32[16,64,1024]{2,1,0:T(8,128)} %bitcast.5, f32[16,64,1024]{2,1,0:T(8,128)} %bitcast.6, f32[4,256,1024]{2,1,0:T(8,128)} %bitcast.7, s32[1]{0:T(128)S(6)} %copy.10.charge_ref, s32[1]{0:T(128)S(6)} %copy.11.sizes_ref), custom_call_target="tpu_custom_call" | custom-call | flops 25769803776 | bytes 12582912 | tf_op jit(solution)/shard_map/pallas_call | solution.py:438
  204.5 1.2 slice_bitcast_fusion
  205.6 1.7 copy.12
  207.3 1.7 copy.13

commit v3 on v2

--- a/solution.py
+++ b/solution.py
@@ -7,7 +7,9 @@
 from jax.sharding import PartitionSpec as P
 
 epsilon = 1e-06
-CHUNKS = 4
+CHUNKS = 8
+X_LAG = 2
+Z_LAG = 4
 F32 = jnp.float32
 BF16 = jnp.bfloat16
 MESH = pl.DeviceIdType.MESH
@@ -25,15 +27,32 @@
 
 
 def kernel(
-    nq, ns, state_ref, l_ref, r_ref, charge_ref, sizes_ref,
+    nq, ns, state_in, l_in, r_in, charge_ref, sizes_ref,
     nv_ref, out_sigma_ref, proj_ref,
-    l_high, l_low, v_high, v_low, p_high, p_low, x_own, x_sent, x_got,
+    state_ref, l_ref, r_ref, l_high, l_low, v_high, v_low, p_high, p_low, x_own, x_sent, x_got,
     x_relay, y_out, y_got, z_out, z_got, t_out, t_got, sig, gathered, klass, op_got, sec_got,
     x_send, x_recv, w_send, w_recv, y_send, y_recv, z_send, z_recv, t_send, t_recv, g_send, g_recv,
     k_send, k_recv, op_send, op_recv, sec_send, sec_recv,
+    in_sem,
 ):
     no, share, n = state_ref.shape
     rq, cq = share // nq, n // nq
+
+    def l_load(q):
+        at = pl.ds(pl.multiple_of(q * rq, rq), rq)
+        return pltpu.make_async_copy(l_in.at[:, at], l_ref.at[:, at], in_sem.at[1 + 2 * q])
+
+    def r_load(q):
+        return pltpu.make_async_copy(r_in.at[q], r_ref.at[q], in_sem.at[2 + 2 * q])
+
+    state_load = pltpu.make_async_copy(state_in, state_ref, in_sem.at[0])
+    state_load.start()
+
+    def load(q, carry):
+        l_load(q).start()
+        r_load(q).start()
+        return carry
+    lax.fori_loop(0, nq, load, 0)
     s = lax.axis_index("sec")
     k = lax.axis_index("op")
     core = k % 2
@@ -167,6 +186,7 @@
         v_high[at], v_low[at] = split(value)
         return total + jnp.sum((value * value).reshape(share // 8, 8, n), axis=0)
 
+    state_load.wait()
     squares = lax.fori_loop(0, no, fill_start, jnp.zeros((8, n), F32))
     start_square = jnp.sum(squares)
 
@@ -193,27 +213,32 @@
 
     for j in range(1, nx):
         x_copy(klass.at[0], klass, k_send, k_recv, j).start()
-    sec_start(0, jnp.full((8, 128), start_square, F32))
+
+    pair = max(1, 256 // cq)
 
     def left_products(first):
-        def body(q, carry):
+        def body(block, carry):
+            base = block * pair
             if first:
-                at = pl.ds(pl.multiple_of(q * rq, rq), rq)
-                high, low = split(l_ref[:, at, :].reshape(no * rq, n))
-                l_high[q] = high
-                l_low[q] = low
-            else:
-                high, low = l_high[q], l_low[q]
-            product = dot3(high, low, v_high[...], v_low[...], ((1,), (0,)))
-            x_own[q] = product
-            if first:
-                right = r_ref[q]
-                x_sent[q] = jnp.where(charge == d, product, right)
-                p_high[q], p_low[q] = split(jnp.where(crossed, product, right))
-
-            start_shift(x_sent if first else x_own, q)
+                for i in range(pair):
+                    l_load(base + i).wait()
+                    r_load(base + i).wait()
+                    at = pl.ds(pl.multiple_of((base + i) * rq, rq), rq)
+                    l_high[base + i], l_low[base + i] = split(l_ref[:, at, :].reshape(no * rq, n))
+            both = pl.ds(base, pair)
+            high, low = l_high[both].reshape(pair * cq, n), l_low[both].reshape(pair * cq, n)
+            wide = dot3(high, low, v_high[...], v_low[...], ((1,), (0,)))
+            for i in range(pair):
+                q = base + i
+                product = wide[i * cq:(i + 1) * cq]
+                x_own[q] = product
+                if first:
+                    right = r_ref[q]
+                    x_sent[q] = jnp.where(charge == d, product, right)
+                    p_high[q], p_low[q] = split(jnp.where(crossed, product, right))
+                start_shift(x_sent if first else x_own, q)
             return carry
-        lax.fori_loop(0, nq, body, 0)
+        lax.fori_loop(0, nq // pair, body, 0)
 
     def t_copy(way, q):
         to = s - 1 if way == 0 else s + 1
@@ -263,33 +288,43 @@
 
     def right_products(first):
         def body(q, carry):
-            @pl.when(relays & (q % 2 == 1))
-            def _():
-                to_relay(x_sent, q).wait_recv()
-                from_relay(q).start()
+            @pl.when(relays & (q < nq // 2))
+            def _():
+                to_relay(x_sent, 2 * q + 1).wait_recv()
+                from_relay(2 * q + 1).start()
 
             @pl.when(has_src)
             def _():
                 shifted(x_sent, q).wait_recv()
             use_own = charge == 0 if first else charge != d
             high, low = split(jnp.where(use_own, x_own[q], x_got[q]))
-            for p in range(nq):
-                block = dot3(high, low, p_high[p], p_low[p], ((1,), (1,)))
-                if first:
-                    block = jnp.where(crossed, block.T, block)
-                y_out[q, :, p * rq:(p + 1) * rq, :] = block.reshape(no, rq, cq)
+            group = max(1, 256 // cq)
+            for start in range(0, nq, group):
+                at = pl.ds(start, group)
+                wide = dot3(
+                    high, low, p_high[at].reshape(group * cq, n), p_low[at].reshape(group * cq, n), ((1,), (1,)))
+                for i in range(group):
+                    p = start + i
+                    block = wide[:, i * cq:(i + 1) * cq]
+                    if first:
+                        block = jnp.where(crossed, block.T, block)
+                    y_out[q, :, p * rq:(p + 1) * rq, :] = block.reshape(no, rq, cq)
 
             for j in range(1, nx):
                 block = y_out.at[q, pl.ds(((x + j) % nx) * 4, 4)]
                 x_copy(block, y_got.at[q], y_send.at[q], y_recv.at[q], j).start()
 
-            @pl.when(q > 0)
-            def _():
-                reduce_x(q - 1)
-
-            @pl.when(q > 1)
-            def _():
-                reduce_z(q - 2)
+            drain(q, 0)
+            return carry
+
+        def drain(q, carry):
+            @pl.when((q >= X_LAG) & (q < nq + X_LAG))
+            def _():
+                reduce_x(q - X_LAG)
+
+            @pl.when(q >= Z_LAG)
+            def _():
+                reduce_z(q - Z_LAG)
             return carry
         lax.fori_loop(0, nq, body, 0)
 
@@ -311,9 +346,7 @@
                 p_high[q], p_low[q] = split(jnp.where(crossed, x_got[q], r_ref[q]))
                 return carry
             lax.fori_loop(0, nq, keep, 0)
-        reduce_x(nq - 1)
-        reduce_z(nq - 2)
-        reduce_z(nq - 1)
+        lax.fori_loop(nq, nq + Z_LAG, drain, 0)
 
     def neighbours_in(first):
         def body(q, carry):
@@ -344,22 +377,30 @@
         return jnp.where(live(k), sig[...], 0.0)
 
     left_products(True)
+    sec_start(0, jnp.full((8, 128), start_square, F32))
     wait_many(klass, k_send, k_recv, nx)
     right_products(True)
     sigma = neighbours_in(True)
 
     gathered[k] = sigma
 
-    def g_copy(dx, dz, dc, to_x, to_z, to_c):
-        block = gathered.at[member(nx - dx, dz, dc)]
+    def g_block(dx, dz, dc, part):
+        block = member(nx - dx, dz, dc)
+        if part is None:
+            return gathered.at[block]
+        return gathered.at[block, pl.ds(part * (share // 2), share // 2)]
+
+    def g_copy(dx, dz, dc, to_x, to_z, to_c, part=None):
+        block = g_block(dx, dz, dc, part)
         slot = ((dx + to_x) % nx) * 4 + ((dz + to_z) % 2) * 2 + (dc + to_c) % 2
+        slot = no + dx if part == 1 else slot
         return pltpu.make_async_remote_copy(
             src_ref=block, dst_ref=block, send_sem=g_send.at[slot], recv_sem=g_recv.at[slot],
             device_id=(s, member(to_x, to_z, to_c)), device_id_type=MESH)
 
-    def g_wait(dx, dz, dc):
-        block = gathered.at[member(nx - dx, dz, dc)]
-        slot = dx * 4 + dz * 2 + dc
+    def g_wait(dx, dz, dc, part=None):
+        block = g_block(dx, dz, dc, part)
+        slot = no + dx if part == 1 else dx * 4 + dz * 2 + dc
         pltpu.make_async_remote_copy(
             src_ref=block, dst_ref=block, send_sem=g_send.at[slot], recv_sem=g_recv.at[slot],
             device_id=(s, member(0, 0, 1)), device_id_type=MESH).wait_recv()
@@ -379,13 +420,17 @@
     op_start(0, jnp.sum(sigma * start_block(k)))
     g_wait(0, 1, 0)
     for step in around:
-        g_start(0, 1, 0, step, 0, 0)
+        g_start(0, 1, 0, step, 0, 0, 0)
     g_start(0, 1, 0, 0, 0, 1)
     sec_start(1, op_finish(0))
-    for dz in (0, 1):
-        for dx in around:
-            g_wait(dx, dz, 0)
-            g_start(dx, dz, 0, 0, 0, 1)
+    for dx in around:
+        g_wait(dx, 0, 0)
+        g_start(dx, 0, 0, 0, 1, 0, 1)
+        g_start(dx, 0, 0, 0, 0, 1)
+    for dx in around:
+        g_wait(dx, 1, 0, 0)
+        g_wait(dx, 1, 0, 1)
+        g_start(dx, 1, 0, 0, 0, 1)
     start_total = sec_finish(0)
     cross_total = sec_finish(1)
     scale = lax.rsqrt(start_total / cells + epsilon)
@@ -407,9 +452,9 @@
         return total + jnp.sum((value * value).reshape(share // 8, 8, n), axis=0)
 
     squares = lax.fori_loop(0, no, fill_residual, jnp.zeros((8, n), F32))
+
+    left_products(False)
     sec_start(2, jnp.full((8, 128), jnp.sum(squares), F32))
-
-    left_products(False)
     right_products(False)
     residual_total = sec_finish(2)
     next_tile = scale * lax.rsqrt(residual_total * (scale * scale) / cells + epsilon)
@@ -434,6 +479,7 @@
     vmem = pltpu.VMEM
     dma = pltpu.SemaphoreType.DMA
     whole = pl.BlockSpec(memory_space=vmem)
+    far = pl.BlockSpec(memory_space=pl.ANY)
     small = pl.BlockSpec(memory_space=pltpu.SMEM)
     nv, sigma, proj = pl.pallas_call(
         functools.partial(kernel, nq, ns),
@@ -442,9 +488,10 @@
             jax.ShapeDtypeStruct((1, share, n), F32),
             jax.ShapeDtypeStruct((8, 128), F32),
         ],
-        in_specs=[whole, whole, whole, small, small],
+        in_specs=[far, far, far, small, small],
         out_specs=[whole, whole, whole],
         scratch_shapes=[
+            vmem((no, share, n), F32), vmem((no, share, n), F32), vmem((nq, cq, n), F32),
             vmem((nq, cq, n), BF16), vmem((nq, cq, n), BF16),
             vmem((n, n), BF16), vmem((n, n), BF16),
             vmem((nq, cq, n), BF16), vmem((nq, cq, n), BF16),
@@ -458,8 +505,9 @@
             vmem((2, no, 8, 128), F32), vmem((4, ns, 8, 128), F32),
             dma((nq,)), dma((nq,)), dma((nq // 2,)), dma((nq // 2,)),
             dma((nq,)), dma((nq,)), dma((nq,)), dma((nq,)),
-            dma((2, nq)), dma((2, nq)), dma((no,)), dma((no,)),
+            dma((2, nq)), dma((2, nq)), dma((no + no // 4,)), dma((no + no // 4,)),
             dma, dma, dma((2,)), dma((2,)), dma((4,)), dma((4,)),
+            dma((1 + 2 * nq,)),
         ],
         compiler_params=pltpu.CompilerParams(
             collective_id=0, has_side_effects=True, vmem_limit_bytes=60 * 1024 * 1024),

time: 209 us -> 193 us (0.923)
  Pallas kernels: 203 us -> 187 us
    pallas_call x1, Pallas kernels: 203 us -> 187 us  [on_device(): pl.pallas_call(functools.partial(kernel, nq, ns), out_shape=[jax.ShapeDty...]
where the time goes in v3:
time: 193 us
  Pallas kernels  187 us (97%)
  local copies, waits for them, and re-layouts  4.53 us (2%)
  between operations  1.93 us (1%)
    pallas_call x1, Pallas kernels, on_device(): pl.pallas_call(functools.partial(kernel, nq, ns), out_shape=[jax.ShapeDty...  187 us

profile of v3, /device:TPU:1, one launch (start us, length us, event | category | flops | bytes accessed | tf_op | source)
XLA Modules:
  0.0 193.2 jit_solution(8152064692951537388)
XLA Ops:
  1.9 186.7 %shard_map.76 = (f32[1,64,1024]{2,1,0:T(8,128)}, f32[1,64,1024]{2,1,0:T(8,128)}, f32[8,128]{1,0:T(8,128)}) custom-call(f32[16,64,1024]{2,1,0:T(8,128)} %bitcast.5, f32[16,64,1024]{2,1,0:T(8,128)} %bitcast.6, f32[8,128,1024]{2,1,0:T(8,128)} %bitcast.7, s32[1]{0:T(128)S(6)} %copy.10.charge_ref, s32[1]{0:T(128)S(6)} %copy.11.sizes_ref), custom_call_target="tpu_custom_call" | custom-call | flops 25769803776 | bytes 12582912 | tf_op jit(solution)/shard_map/pallas_call | solution.py:484
  188.7 1.2 slice_bitcast_fusion
  189.8 1.7 copy.12
  191.5 1.7 copy.13

commit v4 on v3

--- a/solution.py
+++ b/solution.py
@@ -30,7 +30,7 @@
     nq, ns, state_in, l_in, r_in, charge_ref, sizes_ref,
     nv_ref, out_sigma_ref, proj_ref,
     state_ref, l_ref, r_ref, l_high, l_low, v_high, v_low, p_high, p_low, x_own, x_sent, x_got,
-    x_relay, y_out, y_got, z_out, z_got, t_out, t_got, sig, gathered, klass, op_got, sec_got,
+    x_relay, y_out, y_got, z_out, z_got, t_out, t_got, sig, gathered, klass, squares, op_got, sec_got,
     x_send, x_recv, w_send, w_recv, y_send, y_recv, z_send, z_recv, t_send, t_recv, g_send, g_recv,
     k_send, k_recv, op_send, op_recv, sec_send, sec_recv,
     in_sem,
@@ -187,8 +187,8 @@
         return total + jnp.sum((value * value).reshape(share // 8, 8, n), axis=0)
 
     state_load.wait()
-    squares = lax.fori_loop(0, no, fill_start, jnp.zeros((8, n), F32))
-    start_square = jnp.sum(squares)
+    start_squares = lax.fori_loop(0, no, fill_start, jnp.zeros((8, n), F32))
+    start_square = jnp.sum(start_squares)
 
     @pl.when(jnp.logical_not(has_src))
     def _():
@@ -202,7 +202,6 @@
     def _():
         t_got[1] = jnp.zeros(t_got.shape[1:], F32)
 
-    pl.semaphore_wait(barrier, no - 1 + 2 * (ns - 1))
 
     klass[0] = jnp.full((8, 128), jnp.where(crossed, 1.0, 0.0), F32)
 
@@ -211,24 +210,25 @@
             src_ref=source, dst_ref=target.at[j], send_sem=send, recv_sem=recv,
             device_id=(s, member(j, 0, 0)), device_id_type=MESH)
 
-    for j in range(1, nx):
-        x_copy(klass.at[0], klass, k_send, k_recv, j).start()
+    def enter():
+        pl.semaphore_wait(barrier, no - 1 + 2 * (ns - 1))
+        for j in range(1, nx):
+            x_copy(klass.at[0], klass, k_send, k_recv, j).start()
 
     pair = max(1, 256 // cq)
 
     def left_products(first):
-        def body(block, carry):
-            base = block * pair
+        def multiply(base, count):
             if first:
-                for i in range(pair):
+                for i in range(count):
                     l_load(base + i).wait()
                     r_load(base + i).wait()
                     at = pl.ds(pl.multiple_of((base + i) * rq, rq), rq)
                     l_high[base + i], l_low[base + i] = split(l_ref[:, at, :].reshape(no * rq, n))
-            both = pl.ds(base, pair)
-            high, low = l_high[both].reshape(pair * cq, n), l_low[both].reshape(pair * cq, n)
+            some = pl.ds(base, count)
+            high, low = l_high[some].reshape(count * cq, n), l_low[some].reshape(count * cq, n)
             wide = dot3(high, low, v_high[...], v_low[...], ((1,), (0,)))
-            for i in range(pair):
+            for i in range(count):
                 q = base + i
                 product = wide[i * cq:(i + 1) * cq]
                 x_own[q] = product
@@ -236,9 +236,23 @@
                     right = r_ref[q]
                     x_sent[q] = jnp.where(charge == d, product, right)
                     p_high[q], p_low[q] = split(jnp.where(crossed, product, right))
-                start_shift(x_sent if first else x_own, q)
-            return carry
-        lax.fori_loop(0, nq // pair, body, 0)
+
+        def body(block, carry):
+            multiply(block * pair, pair)
+            for i in range(pair):
+                start_shift(x_sent if first else x_own, block * pair + i)
+            return carry
+
+        def single(q, carry):
+            multiply(q, 1)
+            if first:
+                @pl.when(q == 0)
+                def _():
+                    enter()
+            start_shift(x_sent if first else x_own, q)
+            return carry
+        lax.fori_loop(0, pair, single, 0)
+        lax.fori_loop(1, nq // pair, body, 0)
 
     def t_copy(way, q):
         to = s - 1 if way == 0 else s + 1
@@ -412,62 +426,84 @@
         copy.start()
         sends.append(copy)
 
+    op_start(0, jnp.sum(sigma * start_block(k)))
     around = [1, nx - 1] + list(range(2, nx - 1))
     g_start(0, 0, 0, 0, 1, 0)
     for step in around:
         g_start(0, 0, 0, step, 0, 0)
     g_start(0, 0, 0, 0, 0, 1)
-    op_start(0, jnp.sum(sigma * start_block(k)))
+    sec_start(1, op_finish(0))
     g_wait(0, 1, 0)
     for step in around:
         g_start(0, 1, 0, step, 0, 0, 0)
     g_start(0, 1, 0, 0, 0, 1)
-    sec_start(1, op_finish(0))
-    for dx in around:
+    near, last = around[:2], around[2:]
+    for dx in near:
         g_wait(dx, 0, 0)
         g_start(dx, 0, 0, 0, 1, 0, 1)
         g_start(dx, 0, 0, 0, 0, 1)
-    for dx in around:
-        g_wait(dx, 1, 0, 0)
-        g_wait(dx, 1, 0, 1)
-        g_start(dx, 1, 0, 0, 0, 1)
     start_total = sec_finish(0)
     cross_total = sec_finish(1)
     scale = lax.rsqrt(start_total / cells + epsilon)
     rayleigh_one = cross_total * (scale * scale) / cells
     shift_by = jnp.max(rayleigh_one)
-    for dz in (0, 1):
-        for dx in range(nx):
-            g_wait(dx, dz, 1)
-    for copy in sends:
-        copy.wait_send()
 
     def residual_block(block):
         return gathered[block] - shift_by * start_block(block)
 
-    def fill_residual(block, total):
+    def fill_residual(dx, dz, dc):
+        block = member(nx - dx, dz, dc)
         value = residual_block(block)
         at = pl.ds(pl.multiple_of(block * share, share), share)
         v_high[at], v_low[at] = split(value)
-        return total + jnp.sum((value * value).reshape(share // 8, 8, n), axis=0)
-
-    squares = lax.fori_loop(0, no, fill_residual, jnp.zeros((8, n), F32))
+        rows_sum = jnp.sum((value * value).reshape(share // 8, 8, n), axis=0)
+        lanes = [rows_sum[:, i * 128:(i + 1) * 128] for i in range(n // 128)]
+        squares[block] = sum(lanes[1:], lanes[0])
+
+    fill_residual(0, 0, 0)
+    fill_residual(0, 1, 0)
+    for dx in last:
+        g_wait(dx, 0, 0)
+        g_start(dx, 0, 0, 0, 1, 0, 1)
+        g_start(dx, 0, 0, 0, 0, 1)
+    for dx in [0] + near:
+        g_wait(dx, 0, 1)
+        fill_residual(dx, 0, 1)
+        if dx:
+            fill_residual(dx, 0, 0)
+    for dx in around:
+        g_wait(dx, 1, 0, 0)
+        g_wait(dx, 1, 0, 1)
+        g_start(dx, 1, 0, 0, 0, 1)
+        fill_residual(dx, 1, 0)
+        if dx in last:
+            fill_residual(dx, 0, 0)
+    for dx in last:
+        g_wait(dx, 0, 1)
+        fill_residual(dx, 0, 1)
+    for dx in [0] + around:
+        g_wait(dx, 1, 1)
+        fill_residual(dx, 1, 1)
 
     left_products(False)
-    sec_start(2, jnp.full((8, 128), jnp.sum(squares), F32))
+    square = jnp.zeros((8, 128), F32)
+    for i in range(no):
+        square = square + squares[i]
+    sec_start(2, jnp.full((8, 128), jnp.sum(square), F32))
+    for copy in sends:
+        copy.wait_send()
     right_products(False)
     residual_total = sec_finish(2)
     next_tile = scale * lax.rsqrt(residual_total * (scale * scale) / cells + epsilon)
-    next_scale = jnp.max(next_tile)
     sigma = neighbours_in(False)
     residual = residual_block(k)
     op_start(1, jnp.sum(sigma * residual))
-    nv_ref[0] = residual * next_scale
-    out_sigma_ref[0] = sigma * next_scale
+    nv_ref[0] = residual
+    out_sigma_ref[0] = sigma
     sec_start(3, op_finish(1))
     rayleigh_two = sec_finish(3) * (next_tile * next_tile) / cells
     lane = lax.broadcasted_iota(jnp.int32, (8, 128), 1)
-    proj_ref[...] = jnp.where(lane == 0, rayleigh_one, rayleigh_two)
+    proj_ref[...] = jnp.where(lane == 0, rayleigh_one, jnp.where(lane == 1, rayleigh_two, next_tile))
 
 
 def on_device(ns, state, left_ops, right_ops, charge, sizes):
@@ -501,7 +537,7 @@
             vmem((nq, 4, 2, share, cq), F32), vmem((nq, 4, 2, share, cq), F32),
             vmem((2, nq, share, cq), F32), vmem((2, nq, share, cq), F32),
             vmem((share, n), F32), vmem((no, share, n), F32),
-            vmem((no // 4, 8, 128), F32),
+            vmem((no // 4, 8, 128), F32), vmem((no, 8, 128), F32),
             vmem((2, no, 8, 128), F32), vmem((4, ns, 8, 128), F32),
             dma((nq,)), dma((nq,)), dma((nq // 2,)), dma((nq // 2,)),
             dma((nq,)), dma((nq,)), dma((nq,)), dma((nq,)),
@@ -513,7 +549,8 @@
             collective_id=0, has_side_effects=True, vmem_limit_bytes=60 * 1024 * 1024),
         cost_estimate=pl.CostEstimate(flops=24 * n * n * n, bytes_accessed=12 * n * n, transcendentals=0),
     )(state.reshape(no, share, n), left_ops.reshape(no, share, n), right_ops.reshape(nq, cq, n), charge, sizes)
-    return nv, sigma, proj[0, :2]
+    next_scale = proj[0, 2]
+    return nv * next_scale, sigma * next_scale, proj[0, :2]
 
 
 def solution(mesh):

time: 193 us -> 186 us (0.964)
  Pallas kernels: 187 us -> 179 us
  other arithmetic: 0 us -> 2.51 us
  local copies, waits for them, and re-layouts: 4.53 us -> 2.46 us
    pallas_call x1, Pallas kernels: 187 us -> 179 us  [on_device(): pl.pallas_call(functools.partial(kernel, nq, ns), out_shape=[jax.ShapeDty...]
    unnamed x2 -> x0, local copies, waits for them, and re-layouts: 3.34 us -> none
    mul x0 -> x1, other arithmetic: none -> 2.51 us  [on_device(): return (nv * next_scale, sigma * next_scale, proj[0, :2])]
where the time goes in v4:
time: 186 us
  Pallas kernels  179 us (96%)
  other arithmetic  2.51 us (1%)
  local copies, waits for them, and re-layouts  2.46 us (1%)
  between operations  1.93 us (1%)
    pallas_call x1, Pallas kernels, on_device(): pl.pallas_call(functools.partial(kernel, nq, ns), out_shape=[jax.ShapeDty...  179 us

profile of v4, /device:TPU:1, one launch (start us, length us, event | category | flops | bytes accessed | tf_op | source)
XLA Modules:
  0.0 185.5 jit_solution(17871469852457291886)
XLA Ops:
  1.9 178.6 %shard_map.76 = (f32[1,64,1024]{2,1,0:T(8,128)}, f32[1,64,1024]{2,1,0:T(8,128)}, f32[8,128]{1,0:T(8,128)}) custom-call(f32[16,64,1024]{2,1,0:T(8,128)} %bitcast.6, f32[16,64,1024]{2,1,0:T(8,128)} %bitcast.7, f32[8,128,1024]{2,1,0:T(8,128)} %bitcast.8, s32[1]{0:T(128)S(6)} %copy.8.charge_ref, s32[1]{0:T(128)S(6)} %copy.9.sizes_ref), custom_call_target="tpu_custom_call" | custom-call | flops 25769803776 | bytes 12582912 | tf_op jit(solution)/shard_map/pallas_call | solution.py:520
  180.6 1.3 slice.6
  181.8 2.5 %broadcast_multiply_fusion = (f32[1,64,1024]{2,1,0:T(8,128)}, f32[1,64,1024]{2,1,0:T(8,128)}) fusion(f32[1,64,1024]{2,1,0:T(8,128)} %get-tuple-element.8, f32[]{:T(128)} %bitcast.3, f32[1,64,1024]{2,1,0:T(8,128)} %get-tuple-element.6), kind=kLoop, calls=%fused_computation | loop fusion | flops 131072 | bytes 1048580 | tf_op jit(solution)/shard_map/mul | solution.py:553
  184.4 1.2 slice_bitcast_fusion

commit v5 on v4

--- a/solution.py
+++ b/solution.py
@@ -28,7 +28,7 @@
 
 def kernel(
     nq, ns, state_in, l_in, r_in, charge_ref, sizes_ref,
-    nv_ref, out_sigma_ref, proj_ref,
+    nv_ref, out_sigma_ref, proj_ref, scale_ref,
     state_ref, l_ref, r_ref, l_high, l_low, v_high, v_low, p_high, p_low, x_own, x_sent, x_got,
     x_relay, y_out, y_got, z_out, z_got, t_out, t_got, sig, gathered, klass, squares, op_got, sec_got,
     x_send, x_recv, w_send, w_recv, y_send, y_recv, z_send, z_recv, t_send, t_recv, g_send, g_recv,
@@ -442,6 +442,10 @@
         g_wait(dx, 0, 0)
         g_start(dx, 0, 0, 0, 1, 0, 1)
         g_start(dx, 0, 0, 0, 0, 1)
+    for dx in last:
+        g_wait(dx, 0, 0)
+        g_start(dx, 0, 0, 0, 1, 0, 1)
+        g_start(dx, 0, 0, 0, 0, 1)
     start_total = sec_finish(0)
     cross_total = sec_finish(1)
     scale = lax.rsqrt(start_total / cells + epsilon)
@@ -462,10 +466,6 @@
 
     fill_residual(0, 0, 0)
     fill_residual(0, 1, 0)
-    for dx in last:
-        g_wait(dx, 0, 0)
-        g_start(dx, 0, 0, 0, 1, 0, 1)
-        g_start(dx, 0, 0, 0, 0, 1)
     for dx in [0] + near:
         g_wait(dx, 0, 1)
         fill_residual(dx, 0, 1)
@@ -502,8 +502,9 @@
     out_sigma_ref[0] = sigma
     sec_start(3, op_finish(1))
     rayleigh_two = sec_finish(3) * (next_tile * next_tile) / cells
-    lane = lax.broadcasted_iota(jnp.int32, (8, 128), 1)
-    proj_ref[...] = jnp.where(lane == 0, rayleigh_one, jnp.where(lane == 1, rayleigh_two, next_tile))
+    proj_ref[0] = shift_by
+    proj_ref[1] = jnp.max(rayleigh_two)
+    scale_ref[0] = jnp.max(next_tile)
 
 
 def on_device(ns, state, left_ops, right_ops, charge, sizes):
@@ -517,15 +518,16 @@
     whole = pl.BlockSpec(memory_space=vmem)
     far = pl.BlockSpec(memory_space=pl.ANY)
     small = pl.BlockSpec(memory_space=pltpu.SMEM)
-    nv, sigma, proj = pl.pallas_call(
+    nv, sigma, proj, scale = pl.pallas_call(
         functools.partial(kernel, nq, ns),
         out_shape=[
             jax.ShapeDtypeStruct((1, share, n), F32),
             jax.ShapeDtypeStruct((1, share, n), F32),
-            jax.ShapeDtypeStruct((8, 128), F32),
+            jax.ShapeDtypeStruct((2,), F32),
+            jax.ShapeDtypeStruct((1,), F32),
         ],
         in_specs=[far, far, far, small, small],
-        out_specs=[whole, whole, whole],
+        out_specs=[whole, whole, small, small],
         scratch_shapes=[
             vmem((no, share, n), F32), vmem((no, share, n), F32), vmem((nq, cq, n), F32),
             vmem((nq, cq, n), BF16), vmem((nq, cq, n), BF16),
@@ -549,8 +551,7 @@
             collective_id=0, has_side_effects=True, vmem_limit_bytes=60 * 1024 * 1024),
         cost_estimate=pl.CostEstimate(flops=24 * n * n * n, bytes_accessed=12 * n * n, transcendentals=0),
     )(state.reshape(no, share, n), left_ops.reshape(no, share, n), right_ops.reshape(nq, cq, n), charge, sizes)
-    next_scale = proj[0, 2]
-    return nv * next_scale, sigma * next_scale, proj[0, :2]
+    return nv * scale[0], sigma * scale[0], proj
 
 
 def solution(mesh):

time: 186 us -> 184 us (0.989)
  no operation moved by 1% of the time
where the time goes in v5:
time: 184 us
  Pallas kernels  179 us (97%)
  other arithmetic  2.47 us (1%)
  between operations  1.93 us (1%)
    pallas_call x1, Pallas kernels, on_device(): pl.pallas_call(functools.partial(kernel, nq, ns), out_shape=[jax.ShapeDty...  179 us

profile of v5, /device:TPU:1, one launch (start us, length us, event | category | flops | bytes accessed | tf_op | source)
XLA Modules:
  0.0 184.2 jit_solution(1338267891829215690)
XLA Ops:
  1.9 178.6 %shard_map.76 = (f32[1,64,1024]{2,1,0:T(8,128)}, f32[1,64,1024]{2,1,0:T(8,128)}, f32[2]{0:T(128)}, f32[1]{0:T(128)}) custom-call(f32[16,64,1024]{2,1,0:T(8,128)} %bitcast.4, f32[16,64,1024]{2,1,0:T(8,128)} %bitcast.5, f32[8,128,1024]{2,1,0:T(8,128)} %bitcast.6, s32[1]{0:T(128)S(6)} %copy.9.charge_ref, s32[1]{0:T(128)S(6)} %copy.10.sizes_ref), custom_call_target="tpu_custom_call" | custom-call | flops 25769803776 | bytes 12582912 | tf_op jit(solution)/shard_map/pallas_call | solution.py:521
  180.6 2.5 %broadcast_multiply_fusion = (f32[1,64,1024]{2,1,0:T(8,128)}, f32[1,64,1024]{2,1,0:T(8,128)}) fusion(f32[1,64,1024]{2,1,0:T(8,128)} %get-tuple-element.9, f32[]{:T(128)} %bitcast.3, f32[1,64,1024]{2,1,0:T(8,128)} %get-tuple-element.7), kind=kLoop, calls=%fused_computation | loop fusion | flops 131072 | bytes 1048580 | tf_op jit(solution)/shard_map/mul | solution.py:554
  183.1 1.2 copy.11

commit v6 on v5

--- a/solution.py
+++ b/solution.py
@@ -360,7 +360,12 @@
                 p_high[q], p_low[q] = split(jnp.where(crossed, x_got[q], r_ref[q]))
                 return carry
             lax.fori_loop(0, nq, keep, 0)
-        lax.fori_loop(nq, nq + Z_LAG, drain, 0)
+        lax.fori_loop(nq, nq + X_LAG - 1, drain, 0)
+        for q in range(nq + X_LAG - 1 - Z_LAG, nq - 2):
+            reduce_z(q)
+        reduce_x(nq - 1)
+        reduce_z(nq - 2)
+        reduce_z(nq - 1)
 
     def neighbours_in(first):
         def body(q, carry):

time: 184 us -> 184 us (level)
  no operation moved by 1% of the time
where the time goes in v6:
time: 184 us
  Pallas kernels  179 us (97%)
  other arithmetic  2.47 us (1%)
  between operations  1.93 us (1%)
    pallas_call x1, Pallas kernels, on_device(): pl.pallas_call(functools.partial(kernel, nq, ns), out_shape=[jax.ShapeDty...  179 us

profile of v6, /device:TPU:1, one launch (start us, length us, event | category | flops | bytes accessed | tf_op | source)
XLA Modules:
  0.0 184.2 jit_solution(3532883690537936651)
XLA Ops:
  1.9 178.6 %shard_map.76 = (f32[1,64,1024]{2,1,0:T(8,128)}, f32[1,64,1024]{2,1,0:T(8,128)}, f32[2]{0:T(128)}, f32[1]{0:T(128)}) custom-call(f32[16,64,1024]{2,1,0:T(8,128)} %bitcast.4, f32[16,64,1024]{2,1,0:T(8,128)} %bitcast.5, f32[8,128,1024]{2,1,0:T(8,128)} %bitcast.6, s32[1]{0:T(128)S(6)} %copy.9.charge_ref, s32[1]{0:T(128)S(6)} %copy.10.sizes_ref), custom_call_target="tpu_custom_call" | custom-call | flops 25769803776 | bytes 12582912 | tf_op jit(solution)/shard_map/pallas_call | solution.py:526
  180.6 2.5 %broadcast_multiply_fusion = (f32[1,64,1024]{2,1,0:T(8,128)}, f32[1,64,1024]{2,1,0:T(8,128)}) fusion(f32[1,64,1024]{2,1,0:T(8,128)} %get-tuple-element.9, f32[]{:T(128)} %bitcast.3, f32[1,64,1024]{2,1,0:T(8,128)} %get-tuple-element.7), kind=kLoop, calls=%fused_computation | loop fusion | flops 131072 | bytes 1048580 | tf_op jit(solution)/shard_map/mul | solution.py:559
  183.1 1.2 copy.11
